TPU v7x, 256 devices: a whole 4x4x8 slice. The times are simulated.
256 devices in a mesh: dp: 32 (over z, y_lo, core), tensor: 8 (over x, y_hi).
Axes of the slice: x: 4, y: 4 (y_hi: 2, y_lo: 2; y = y_hi * 2 + y_lo), z: 8, core: 2. Of those that a mesh axis runs over, the one named last changes fastest.
Arguments:
- layer_input: bfloat16 [4096, 8192], P('dp'), as said below
- gate_pre: bfloat16 [4096, 28672], P('dp', 'tensor'), as said below
- up_pre: bfloat16 [4096, 28672], P('dp', 'tensor'), as said below
- hidden_cot: bfloat16 [4096, 28672], P('dp', 'tensor'), as said below
- other_norms: float32 [64, 128], P('dp', 'tensor'), as said below
- noise_gate: bfloat16 [8192, 28672], P('dp', 'tensor'), may hold values from -3 to 3
Outputs:
- gate_grad: float32 [8192, 28672], P('dp', 'tensor')
Inputs may be any that keep to these rules, and one draw needn't show every extreme that they name: `layer_input`: inputs of the layer, of order one. `gate_pre`: pre-activations of the gate. `up_pre`: pre-activations of the up projection. `hidden_cot`: a cotangent of the hidden units. `other_norms`: positive squared norms.
All inputs are finite; a program needn't handle non-finite values.
Results may differ from a plain program's by a relative error of at most 0.0025.
Values may be sent and summed in bfloat16 or wider, within the bound.
A program may use at most 128 MiB of HBM per device.

v0:
```python
import math

import jax
import jax.numpy as jnp
from jax import lax
from jax.sharding import PartitionSpec as P

D = 8192
FF = 28672
SEQ = 64


clip_ratio = 0.045


def shards(layer_input, gate_pre, up_pre, hidden_cot, other_norms, noise_gate):
    tokens = layer_input.shape[0]
    examples = tokens // SEQ
    gate = gate_pre.astype(jnp.float32)
    upper = up_pre.astype(jnp.float32)
    cotan = hidden_cot.astype(jnp.float32)
    sigmoid_gate = jax.nn.sigmoid(gate)
    activated = gate * sigmoid_gate
    slope = sigmoid_gate * (1.0 + gate * (1.0 - sigmoid_gate))
    gate_cot = (cotan * upper * slope).astype(jnp.bfloat16)
    up_cot = (cotan * activated).astype(jnp.bfloat16)
    shaped = layer_input.reshape(examples, SEQ, D)
    gram_x = jnp.einsum("etd,esd->ets", shaped, shaped, preferred_element_type=jnp.float32)
    gate_rows = gate_cot.reshape(examples, SEQ, -1)
    up_rows = up_cot.reshape(examples, SEQ, -1)
    gram_cot = jnp.einsum("etf,esf->ets", gate_rows, gate_rows, preferred_element_type=jnp.float32)
    gram_cot = gram_cot + jnp.einsum(
        "etf,esf->ets", up_rows, up_rows, preferred_element_type=jnp.float32
    )
    partial_norm = jnp.sum(gram_x * gram_cot, axis=(1, 2)) + jnp.sum(other_norms, axis=1)
    sq_norm = lax.psum(partial_norm, "tensor")
    clip_bound = clip_ratio * math.sqrt(SEQ * D * FF)
    factor = clip_bound / jnp.maximum(jnp.sqrt(sq_norm), clip_bound)
    clipped = (gate_rows.astype(jnp.float32) * factor[:, None, None]).astype(jnp.bfloat16)
    clipped = clipped.reshape(tokens, -1)
    columns = lax.all_to_all(layer_input, "dp", split_axis=1, concat_axis=0, tiled=True)
    grad = lax.dot_general(
        columns,
        lax.all_gather(clipped, "dp", axis=0, tiled=True),
        (((0,), (0,)), ((), ())),
        preferred_element_type=jnp.float32,
    )
    return grad + noise_gate.astype(jnp.float32)


def solution(mesh):
    placed = (
        P("dp", None),
        P("dp", "tensor"),
        P("dp", "tensor"),
        P("dp", "tensor"),
        P("dp", "tensor"),
        P("dp", "tensor"),
    )
    return jax.shard_map(
        shards, mesh=mesh, in_specs=placed, out_specs=P("dp", "tensor"), check_vma=False
    )
```

profile of v0, /device:TPU:1, one launch (start us, length us, event | category | flops | bytes accessed | tf_op | source)
XLA Modules:
  0.0 272.9 jit_solution(4169151111773700769)
XLA Ops:
  6.5 0.0 all-gather.2.cloned.1.call-start
  6.5 0.0 copy-start.1
  6.5 0.0 copy-start.2
  6.5 0.0 copy-start.3
  6.5 3.1 %fusion.11 = f32[2,64,64]{2,1,0:T(8,128)S(1)} fusion(bf16[2,64,8192]{2,1,0:T(8,128)(2,1)} %bitcast.18), kind=kOutput, calls=%fused_computation.20 | convolution fusion | flops 134217728 | bytes 2129920 | tf_op jit(solution)/shard_map/etd,esd->ets/dot_general | solution.py:28
  9.6 0.0 copy-done.1
  9.6 0.0 copy-done.2
  9.6 0.0 copy-done.3
  9.6 1.0 fusion.3
  10.6 0.0 copy-start.4
  10.6 0.4 fusion.12
  11.0 0.3 copy-done.4
  11.3 0.1 reduce_sum.19
  11.4 0.5 fusion.10
  11.9 0.0 copy-start
  11.9 21.5 %psum.7 = f32[2]{0:T(128)S(1)} all-reduce(f32[2]{0:T(128)S(1)} %add.20), channel_id=1, replica_groups=mesh['dp'=32,'tensor'=8] {'tensor'}, use_global_device_ids=true, to_apply=%region_2.0 | all-reduce | flops 2 | bytes 16 | tf_op jit(solution)/shard_map/psum | solution.py:36
  33.5 0.1 mul.41
  33.5 0.1 mul.42
  33.6 1.2 multiply_convert_fusion
  34.8 0.0 all-gather.2.cloned.1.call-update
  34.9 0.0 copy-done
  34.9 2.4 copy.11
  37.3 13.2 %all-to-all-start = ((bf16[128,32,256]{0,2,1:T(8,128)(2,1)}), bf16[128,32,256]{0,2,1:T(8,128)(2,1)S(1)}, u32[]{:S(2)}, u32[]{:S(2)}) async-start(bf16[128,32,256]{0,2,1:T(8,128)(2,1)} %bitcast.21), calls=%async_computation | async-start | bytes 4194304 | tf_op jit(solution)/shard_map/all_to_all | solution.py:41
  50.5 3.8 %copy.13 = bf16[256,3584]{0,1:T(8,128)(2,1)} copy(bf16[256,3584]{1,0:T(8,128)(2,1)} %param.11) | data formatting | bytes 3670016 | tf_op args[5]
  54.3 69.9 %all-to-all-done = bf16[128,32,256]{0,2,1:T(8,128)(2,1)S(1)} async-done(((bf16[128,32,256]{0,2,1:T(8,128)(2,1)}), bf16[128,32,256]{0,2,1:T(8,128)(2,1)S(1)}, u32[]{:S(2)}, u32[]{:S(2)}) %all-to-all-start) | async-done | bytes 2097184 | tf_op jit(solution)/shard_map/all_to_all | solution.py:41
  124.3 2.9 %copy.12 = bf16[32,128,256]{2,1,0:T(8,128)(2,1)} copy(bf16[32,128,256]{1,2,0:T(8,128)(2,1)S(1)} %bitcast.20) | data formatting | bytes 4194304 | tf_op jit(solution)/shard_map/all_to_all | solution.py:41
  127.1 118.1 %all-gather.2.cloned.1.call-done = bf16[4096,3584]{1,0:T(8,128)(2,1)} async-done(((bf16[128,3584]{1,0:T(8,128)(2,1)}), bf16[4096,3584]{1,0:T(8,128)(2,1)}) %all-gather.2.cloned.1.call-update) | async-done | bytes 29360144 | tf_op jit(solution)/shard_map/all_gather | solution.py:44
  245.2 15.7 %fusion = f32[256,3584]{0,1:T(8,128)} fusion(bf16[4096,3584]{1,0:T(8,128)(2,1)} %all-gather.2.cloned.1.call-done, bf16[4096,256]{1,0:T(8,128)(2,1)} %bitcast.23, bf16[256,3584]{0,1:T(8,128)(2,1)} %copy.13), kind=kOutput, calls=%fused_computation.1 | convolution fusion | flops 7518027776 | bytes 36962304 | tf_op jit(solution)/shard_map/dot_general | solution.py:42
  260.9 5.1 %copy.14 = f32[256,3584]{1,0:T(8,128)} copy(f32[256,3584]{0,1:T(8,128)} %fusion) | data formatting | bytes 7340032 | tf_op jit(solution)/shard_map/add | solution.py:48
  (2 shorter events, 0.0 us)
Async XLA Ops:
  6.5 238.7 %all-gather.2.cloned.1.call-start = ((), (), s32[]{:S(2)}) async-start(), calls=%async_computation.1 | async-start | bytes 30277632 | tf_op jit(solution)/shard_map/all_gather | solution.py:44
  6.5 3.1 %copy-start.1 = (bf16[128,3584]{1,0:T(8,128)(2,1)S(1)}, bf16[128,3584]{1,0:T(8,128)(2,1)}, u32[]{:S(2)}) copy-start(bf16[128,3584]{1,0:T(8,128)(2,1)} %param.9) | copy-start | bytes 2752516
  6.5 3.1 %copy-start.2 = (bf16[128,3584]{1,0:T(8,128)(2,1)S(1)}, bf16[128,3584]{1,0:T(8,128)(2,1)}, u32[]{:S(2)}) copy-start(bf16[128,3584]{1,0:T(8,128)(2,1)} %param.7) | copy-start | bytes 2752516
  6.5 3.1 %copy-start.3 = (bf16[128,3584]{1,0:T(8,128)(2,1)S(1)}, bf16[128,3584]{1,0:T(8,128)(2,1)}, u32[]{:S(2)}) copy-start(bf16[128,3584]{1,0:T(8,128)(2,1)} %param.8) | copy-start | bytes 2752516
  10.6 0.7 copy-start.4
  11.9 23.0 %copy-start = (bf16[128,8192]{1,0:T(8,128)(2,1)S(1)}, bf16[128,8192]{1,0:T(8,128)(2,1)}, u32[]{:S(2)}) copy-start(bf16[128,8192]{1,0:T(8,128)(2,1)} %param.6) | copy-start | bytes 6291460
  37.3 87.0 %all-to-all-start = ((bf16[128,32,256]{0,2,1:T(8,128)(2,1)}), bf16[128,32,256]{0,2,1:T(8,128)(2,1)S(1)}, u32[]{:S(2)}, u32[]{:S(2)}) async-start(bf16[128,32,256]{0,2,1:T(8,128)(2,1)} %bitcast.21), calls=%async_computation | async-start | bytes 4194304 | tf_op jit(solution)/shard_map/all_to_all | solution.py:41
Sparse Core Ops, SparseCore 0:
  35.0 210.1 all-gather.1
where the time goes:
time: 273 us
  waiting for transfers between devices  188 us (69%)
  blocking collectives  21.5 us (8%)
  matrix products  19.6 us (7%)
  local copies, waits for them, and re-layouts  14.7 us (5%)
  between operations  13.5 us (5%)
  starting transfers between devices  13.2 us (5%)
    all_gather x1, waiting for transfers between devices, shards(): lax.all_gather(clipped, 'dp', axis=0, tiled=True)  118 us
    all_to_all x1, waiting for transfers between devices, shards(): lax.all_to_all(layer_input, 'dp', split_axis=1, concat_axis=0, tiled=True)  69.9 us
    psum x1, blocking collectives, shards(): sq_norm = lax.psum(partial_norm, 'tensor')  21.5 us
    dot_general x1, matrix products, shards(): lax.dot_general(columns, lax.all_gather(clipped, 'dp', axis=0, tiled=True...  15.7 us
    all_to_all x1, starting transfers between devices, shards(): lax.all_to_all(layer_input, 'dp', split_axis=1, concat_axis=0, tiled=True)  13.2 us
    unnamed x12, local copies, waits for them, and re-layouts  6.6 us
  transfers between devices with their start and end apart: 2, of which 2 were waited for; matrix products, arithmetic and copies ran while one was open for 3% of the time, Pallas kernels for 0%

commit v1 on v0

v1 whole, which is shorter than its diff:
```python
import math

import jax
import jax.numpy as jnp
from jax import lax
from jax.experimental import pallas as pl
from jax.experimental.pallas import tpu as pltpu
from jax.sharding import PartitionSpec as P

D = 8192
FF = 28672
SEQ = 64
clip_ratio = 0.045
clip_bound = clip_ratio * math.sqrt(SEQ * D * FF)

Z = 8
Q = 4
XN = 4
T = 8
TOK = 128
COLS = 3584
PART = COLS // Q
W = 128
J = PART // W
ROWS = 1024
OWN = ROWS // Q
LANES = Z * TOK
HALF = LANES // 2
MESH = pl.DeviceIdType.MESH
f32 = jnp.float32
bf16 = jnp.bfloat16


def aligned(value, to=128):
    return pl.multiple_of(value, to)


def kernel(
    x_hbm, g_hbm, u_hbm, c_hbm, other_ref, out_ref,
    x_v, g_v, u_v, c_v, gc, uc, cb, cs, xt, xs, ob, gram, pn, fac,
    in_sem, xz_s, xz_r, xa_s, xa_r, yb_s, yb_r, ya_s, ya_r, xb_s, xb_r, co_s, co_r,
    qa_s, qa_r, rp_s, rp_r, rm_s, rm_r, pn_s, pn_r, fq_s, fq_r, fz_s, fz_r, out_s, out_r, own_s,
):
    dp = lax.axis_index("dp")
    tn = lax.axis_index("tensor")
    z, q = lax.div(dp, Q), lax.rem(dp, Q)
    ylo, core = lax.div(q, 2), lax.rem(q, 2)
    x, yhi = lax.div(tn, 2), lax.rem(tn, 2)
    yy = yhi * 2 + ylo
    xrow = aligned(x * TOK)

    def zq(zd, qd):
        return (zd * Q + qd, tn)

    def x_peer(off):
        return (dp, lax.rem(x + off, XN) * 2 + yhi)

    def y_peer(off):
        to = lax.rem(yy + off, 4)
        return (z * Q + lax.rem(to, 2) * 2 + core, x * 2 + lax.div(to, 2))

    def z_peer(off):
        return zq(lax.rem(z + off, Z), q)

    def q_peer(off):
        return zq(z, lax.rem(q + off, Q))

    def t_peer(off):
        return (dp, lax.rem(tn + off, T))

    core_peer = zq(z, ylo * 2 + 1 - core)

    def remote(src, dst, send, recv, device):
        return pltpu.make_async_remote_copy(
            src_ref=src, dst_ref=dst, send_sem=send, recv_sem=recv,
            device_id=device, device_id_type=MESH,
        )

    loads = [
        pltpu.make_async_copy(src, dst, in_sem.at[i])
        for i, (src, dst) in enumerate(((x_hbm, x_v), (g_hbm, g_v), (u_hbm, u_v), (c_hbm, c_v)))
    ]
    for load in loads:
        load.start()

    barrier = pltpu.get_barrier_semaphore()

    def greet(device):
        pl.semaphore_signal(barrier, inc=1, device_id=device, device_id_type=MESH)

    for off in range(1, Q):
        greet(q_peer(off))
    for off in range(1, Z):
        greet(z_peer(off))
    for off in range(1, T):
        greet(t_peer(off))
    greet((z * Q + (1 - ylo) * 2 + core, x * 2 + 1 - yhi))

    loads[0].wait()

    def turn(zd, _):
        at = aligned(zd * ROWS + yhi * (ROWS // 2) + x * TOK)
        xs[zd] = x_v[:, pl.ds(at, TOK)].T
        return 0

    lax.fori_loop(0, Z, turn, 0)
    mine = xt.at[yhi, pl.ds(xrow, TOK), pl.ds(aligned(q * LANES + z * TOK), TOK)]
    mine[...] = xs[z]

    pl.semaphore_wait(barrier, (Q - 1) + (Z - 1) + (T - 1) + 1)

    def x_z(off):
        return remote(xs.at[lax.rem(z + off, Z)], mine, xz_s.at[off], xz_r.at[off], z_peer(off))

    for off in range(1, Z):
        x_z(off).start()

    for load in loads[1:]:
        load.wait()

    def quad(j, off):
        to = lax.rem(q + off, Q)
        return remote(
            gc.at[:, pl.ds(aligned(to * PART + j * W), W)], cb.at[j, q, z],
            qa_s.at[j, off], qa_r.at[j, off], q_peer(off),
        )

    def cotangents(j):
        for part in range(Q):
            at = pl.ds(aligned(part * PART + j * W), W)
            gate = g_v[:, at].astype(f32)
            upper = u_v[:, at].astype(f32)
            cotan = c_v[:, at].astype(f32)
            sig = jax.nn.sigmoid(gate)
            slope = sig * (1.0 + gate * (1.0 - sig))
            gc[:, at] = (cotan * upper * slope).astype(bf16)
            uc[:, at] = (cotan * (gate * sig)).astype(bf16)
        for off in range(1, Q):
            quad(j, off).start()
        cb[j, q, z] = gc[:, pl.ds(aligned(q * PART + j * W), W)]

    def hop_plus(h, j):
        src = lax.rem(z + Z - (h - 1), Z)
        block = cb.at[j, :, src] if h < 4 else cb.at[j, pl.ds(0, 2), src]
        return remote(block, block, rp_s.at[h - 1, j], rp_r.at[h - 1, j], z_peer(1))

    def hop_minus(h, j):
        src = lax.rem(z + (h - 1), Z)
        block = cb.at[j, :, src] if h < 4 else cb.at[j, pl.ds(2, 2), src]
        return remote(block, block, rm_s.at[h - 1, j], rm_r.at[h - 1, j], z_peer(Z - 1))

    def first_hop(j):
        for off in range(1, Q):
            quad(j, off).wait_recv()
        hop_plus(1, j).start()
        hop_minus(1, j).start()

    cotangents(0)

    def produce(j, _):
        cotangents(j)
        first_hop(j - 1)
        return 0

    lax.fori_loop(1, J, produce, 0)
    first_hop(J - 1)

    cross = (((1,), (1,)), ((), ()))
    gram[...] = jnp.zeros_like(gram)

    def gram_x(k, _):
        part = x_v[:, pl.ds(aligned(k * 1024), 1024)]
        gram[0] += lax.dot_general(part, part, cross, preferred_element_type=f32)
        return 0

    lax.fori_loop(0, D // 1024, gram_x, 0)

    def gram_cot(k, _):
        at = pl.ds(aligned(k * 512), 512)
        gate, upper = gc[:, at], uc[:, at]
        gram[1] += lax.dot_general(gate, gate, cross, preferred_element_type=f32)
        gram[1] += lax.dot_general(upper, upper, cross, preferred_element_type=f32)
        return 0

    lax.fori_loop(0, COLS // 512, gram_cot, 0)

    for e in range(TOK // SEQ):
        at = slice(e * SEQ, (e + 1) * SEQ)
        ghost = jnp.sum(gram[0, at, at] * gram[1, at, at], axis=1, keepdims=True)
        ghost = jnp.sum(ghost, axis=0, keepdims=True)
        rest = jnp.sum(other_ref[e : e + 1, :], axis=1, keepdims=True)
        pn[0, e : e + 1, :] = jnp.broadcast_to(ghost + rest, (1, 128))
    pn[0, 2:8, :] = jnp.zeros((6, 128), f32)

    def norms(off):
        return remote(pn.at[0], pn.at[off], pn_s.at[off], pn_r.at[off], t_peer(off))

    for off in range(1, T):
        norms(off).start()

    def x_a(off):
        part = xt.at[yhi, pl.ds(xrow, TOK), pl.ds(aligned(q * LANES), HALF)]
        return remote(part, part, xa_s.at[off], xa_r.at[off], x_peer(off))

    def y_b(off):
        part = xt.at[yhi, pl.ds(xrow, TOK), pl.ds(aligned(q * LANES + HALF), HALF)]
        return remote(part, part, yb_s.at[off], yb_r.at[off], y_peer(off))

    def y_a(off):
        part = xt.at[yhi, :, pl.ds(aligned(q * LANES), HALF)]
        return remote(part, part, ya_s.at[off], ya_r.at[off], y_peer(off))

    def x_b(off, lo):
        part = xt.at[:, pl.ds(xrow, TOK), pl.ds(aligned((lo * 2 + core) * LANES + HALF), HALF)]
        return remote(part, part, xb_s.at[lo, off], xb_r.at[lo, off], x_peer(off))

    def swap(half, lo):
        part = xt.at[:, :, pl.ds(aligned((lo * 2 + core) * LANES + half * HALF), HALF)]
        return remote(part, part, co_s.at[half, lo], co_r.at[half, lo], core_peer)

    for off in range(1, Z):
        x_z(off).wait_recv()
    for off in range(1, XN):
        x_a(off).start()
        y_b(off).start()

    def second_hop(j, _):
        hop_plus(1, j).wait_recv()
        hop_plus(2, j).start()
        hop_minus(1, j).wait_recv()
        hop_minus(2, j).start()
        return 0

    lax.fori_loop(0, J, second_hop, 0)

    for off in range(1, T):
        norms(off).wait_recv()
    total = jnp.zeros((8, 128), f32)
    for t in range(T):
        total = total + pn[lax.rem(tn + T - t, T)]
    fac[z, q] = clip_bound / jnp.maximum(jnp.sqrt(total), clip_bound)

    def factor_q(off):
        return remote(fac.at[z, q], fac.at[z, q], fq_s.at[off], fq_r.at[off], q_peer(off))

    def factor_z(off):
        return remote(fac.at[z], fac.at[z], fz_s.at[off], fz_r.at[off], z_peer(off))

    for off in range(1, Q):
        factor_q(off).start()

    for off in range(1, XN):
        x_a(off).wait_recv()
        y_b(off).wait_recv()
    for off in range(1, XN):
        y_a(off).start()
        for lo in range(2):
            x_b(off, lo).start()

    for off in range(1, Q):
        factor_q(off).wait_recv()
    for off in range(1, Z):
        factor_z(off).start()
    for off in range(1, Z):
        factor_z(off).wait_recv()

    def scale(j, src):
        for part in range(Q):
            for e in range(TOK // SEQ):
                block = cb[j, part, src, e * SEQ : (e + 1) * SEQ, :].astype(f32)
                block = block * fac[src, part, e : e + 1, :]
                at = aligned((part * Z + src) * TOK + e * SEQ, SEQ)
                cs[j, pl.ds(at, SEQ), :] = block.astype(bf16)

    def third_hop(j, _):
        hop_plus(2, j).wait_recv()
        hop_plus(3, j).start()
        hop_minus(2, j).wait_recv()
        hop_minus(3, j).start()
        for off in (0, 1, Z - 1):
            scale(j, lax.rem(z + off, Z))
        return 0

    lax.fori_loop(0, J, third_hop, 0)

    for off in range(1, XN):
        y_a(off).wait_recv()
    for lo in range(2):
        swap(0, lo).start()
    for off in range(1, XN):
        for lo in range(2):
            x_b(off, lo).wait_recv()
    for lo in range(2):
        swap(1, lo).start()

    def fourth_hop(j, _):
        hop_plus(3, j).wait_recv()
        hop_plus(4, j).start()
        hop_minus(3, j).wait_recv()
        hop_minus(4, j).start()
        for off in (2, 3, Z - 3, Z - 2):
            scale(j, lax.rem(z + off, Z))
        return 0

    lax.fori_loop(0, J, fourth_hop, 0)

    for half in range(2):
        for lo in range(2):
            swap(half, lo).wait_recv()

    def place(j, part):
        return out_ref.at[:, pl.ds(aligned(part * PART + j * W), W)]

    def give(j, off):
        to = lax.rem(q + off, Q)
        return remote(
            ob.at[j, to], place(j, q), out_s.at[j, off], out_r.at[j, off], q_peer(off)
        )

    def keep(j):
        return pltpu.make_async_copy(ob.at[j, q], place(j, q), own_s.at[j])

    def multiply(j, _):
        hop_plus(4, j).wait_recv()
        hop_minus(4, j).wait_recv()
        scale(j, lax.rem(z + 4, Z))
        for half in range(2):
            grad = jnp.dot(xt[half], cs[j], preferred_element_type=f32).astype(bf16)
            ob[j, 2 * half] = grad[:OWN]
            ob[j, 2 * half + 1] = grad[OWN:]
        for off in range(1, Q):
            give(j, off).start()
        keep(j).start()
        return 0

    lax.fori_loop(0, J, multiply, 0)

    for off in range(1, Z):
        x_z(off).wait_send()
        factor_z(off).wait_send()
    for off in range(1, T):
        norms(off).wait_send()
    for off in range(1, Q):
        x_a(off).wait_send()
        y_b(off).wait_send()
        y_a(off).wait_send()
        for lo in range(2):
            x_b(off, lo).wait_send()
        factor_q(off).wait_send()
    for half in range(2):
        for lo in range(2):
            swap(half, lo).wait_send()

    def finish(j, _):
        for off in range(1, Q):
            quad(j, off).wait_send()
        for h in range(1, 5):
            hop_plus(h, j).wait_send()
            hop_minus(h, j).wait_send()
        for off in range(1, Q):
            give(j, off).wait_send()
            give(j, off).wait_recv()
        keep(j).wait()
        return 0

    lax.fori_loop(0, J, finish, 0)


def shards(layer_input, gate_pre, up_pre, hidden_cot, other_norms, noise_gate):
    dma = pltpu.SemaphoreType.DMA
    anywhere = pl.BlockSpec(memory_space=pl.ANY)
    grad = pl.pallas_call(
        kernel,
        out_shape=jax.ShapeDtypeStruct((OWN, COLS), bf16),
        in_specs=[anywhere] * 4 + [pl.BlockSpec(memory_space=pltpu.VMEM)],
        out_specs=anywhere,
        scratch_shapes=[
            pltpu.VMEM((TOK, D), bf16),
            pltpu.VMEM((TOK, COLS), bf16),
            pltpu.VMEM((TOK, COLS), bf16),
            pltpu.VMEM((TOK, COLS), bf16),
            pltpu.VMEM((TOK, COLS), bf16),
            pltpu.VMEM((TOK, COLS), bf16),
            pltpu.VMEM((J, Q, Z, TOK, W), bf16),
            pltpu.VMEM((J, Q * Z * TOK, W), bf16),
            pltpu.VMEM((2, ROWS // 2, Q * LANES), bf16),
            pltpu.VMEM((Z, TOK, TOK), bf16),
            pltpu.VMEM((J, Q, OWN, W), bf16),
            pltpu.VMEM((2, TOK, TOK), f32),
            pltpu.VMEM((T, 8, 128), f32),
            pltpu.VMEM((Z, Q, 8, 128), f32),
            dma((4,)),
            dma((Z,)), dma((Z,)),
            dma((4,)), dma((4,)), dma((4,)), dma((4,)), dma((4,)), dma((4,)),
            dma((2, 4)), dma((2, 4)), dma((2, 2)), dma((2, 2)),
            dma((J, Q)), dma((J, Q)),
            dma((4, J)), dma((4, J)), dma((4, J)), dma((4, J)),
            dma((T,)), dma((T,)), dma((Q,)), dma((Q,)), dma((Z,)), dma((Z,)),
            dma((J, Q)), dma((J, Q)), dma((J,)),
        ],
        compiler_params=pltpu.CompilerParams(
            collective_id=0, has_side_effects=True, vmem_limit_bytes=56 * 1024 * 1024
        ),
        cost_estimate=pl.CostEstimate(
            flops=2 * 4096 * 256 * 3584, bytes_accessed=8 * 1024 * 1024, transcendentals=128 * 3584
        ),
        name="clipped_gradient",
    )(layer_input, gate_pre, up_pre, hidden_cot, other_norms)
    return grad.astype(f32) + noise_gate.astype(f32)


def solution(mesh):
    placed = (
        P("dp", None),
        P("dp", "tensor"),
        P("dp", "tensor"),
        P("dp", "tensor"),
        P("dp", "tensor"),
        P("dp", "tensor"),
    )
    return jax.shard_map(
        shards, mesh=mesh, in_specs=placed, out_specs=P("dp", "tensor"), check_vma=False
    )
```

time: 273 us -> 114 us (0.42)
  waiting for transfers between devices: 188 us -> 0 us
  Pallas kernels: 0 us -> 110 us
  blocking collectives: 21.5 us -> 0 us
  matrix products: 19.6 us -> 0 us
  local copies, waits for them, and re-layouts: 14.7 us -> 0.01 us
  between operations: 13.5 us -> 0.02 us
  starting transfers between devices: 13.2 us -> 0 us
    all_gather x1 -> x0, waiting for transfers between devices: 118 us -> none  [shards(): lax.all_gather(clipped, 'dp', axis=0, tiled=True)]
    pallas_call x0 -> x1, Pallas kernels: none -> 110 us  [shards(): pl.pallas_call(kernel, out_shape=jax.ShapeDtypeStruct((OWN, COLS), bf16),...]
    all_to_all x1 -> x0, waiting for transfers between devices: 69.9 us -> none  [shards(): lax.all_to_all(layer_input, 'dp', split_axis=1, concat_axis=0, tiled=True)]
    psum x1 -> x0, blocking collectives: 21.5 us -> none  [shards(): sq_norm = lax.psum(partial_norm, 'tensor')]
    dot_general x4 -> x0, matrix products: 19.6 us -> none  [the longest x1 15.7 us: shards(): lax.dot_general(columns, lax.all_gather(clipped, 'dp', axis=0, tiled=True...]
    all_to_all x1 -> x0, starting transfers between devices: 13.2 us -> none  [shards(): lax.all_to_all(layer_input, 'dp', split_axis=1, concat_axis=0, tiled=True)]
    unnamed x12 -> x2, local copies, waits for them, and re-layouts: 6.6 us -> 0.01 us
    add x1 -> x0, local copies, waits for them, and re-layouts: 5.11 us -> none  [shards(): return grad + noise_gate.astype(jnp.float32)]
  transfers between devices with their start and end apart: 2 -> 0, of which waited for: 2 -> 0; matrix products, arithmetic and copies ran while one was open for 3% -> 0% of each run, Pallas kernels for 0% -> 0%
where the time goes in v1:
time: 114 us
  Pallas kernels  110 us (96%)
  other arithmetic  3.86 us (3%)
    pallas_call x1, Pallas kernels, shards(): pl.pallas_call(kernel, out_shape=jax.ShapeDtypeStruct((OWN, COLS), bf16),...  110 us
    add x1, other arithmetic, shards(): return grad.astype(f32) + noise_gate.astype(f32)  3.86 us

profile of v1, /device:TPU:1, one launch (start us, length us, event | category | flops | bytes accessed | tf_op | source)
XLA Modules:
  0.0 113.9 jit_solution(17755973953220239673)
XLA Ops:
  0.0 0.0 copy-start
  0.0 110.1 %clipped_gradient.1 = bf16[256,3584]{1,0:T(8,128)(2,1)} custom-call(bf16[128,8192]{1,0:T(8,128)(2,1)} %x_hbm.1, bf16[128,3584]{1,0:T(8,128)(2,1)} %g_hbm.1, bf16[128,3584]{1,0:T(8,128)(2,1)} %u_hbm.1, bf16[128,3584]{1,0:T(8,128)(2,1)} %c_hbm.1, f32[2,16]{1,0:T(2,128)} %other_ref.1), custom_call_target="tpu_custom_call" | custom-call | flops 7516192768 | bytes 8388608 | tf_op jit(solution)/shard_map/clipped_gradient/pallas_call | solution.py:372
  110.1 0.0 copy-done
  110.1 3.9 %convert_add_fusion = f32[256,3584]{1,0:T(8,128)} fusion(bf16[256,3584]{1,0:T(8,128)(2,1)S(1)} %copy-done, bf16[256,3584]{1,0:T(8,128)(2,1)} %clipped_gradient.1), kind=kLoop, calls=%fused_computation | loop fusion | flops 2752512 | bytes 7340032 | tf_op jit(solution)/shard_map/add | solution.py:409
Async XLA Ops:
  0.0 110.1 %copy-start = (bf16[256,3584]{1,0:T(8,128)(2,1)S(1)}, bf16[256,3584]{1,0:T(8,128)(2,1)}, u32[]{:S(2)}) copy-start(bf16[256,3584]{1,0:T(8,128)(2,1)} %param.11) | copy-start | bytes 5505028

commit v2 on v1

v2 whole, which is shorter than its diff:
```python
import math

import jax
import jax.numpy as jnp
from jax import lax
from jax.experimental import pallas as pl
from jax.experimental.pallas import tpu as pltpu
from jax.sharding import PartitionSpec as P

D = 8192
FF = 28672
SEQ = 64
clip_ratio = 0.045
clip_bound = clip_ratio * math.sqrt(SEQ * D * FF)

Z = 8
Q = 4
XN = 4
T = 8
TOK = 128
COLS = 3584
PART = COLS // Q
W = 128
J = PART // W
ROWS = 1024
OWN = ROWS // Q
A, B = pl.ds(0, Z // 2), pl.ds(Z // 2, Z // 2)
LAG = 2
AHEAD = 3
MESH = pl.DeviceIdType.MESH
f32 = jnp.float32
bf16 = jnp.bfloat16


def aligned(value, to=128):
    return pl.multiple_of(value, to)


def tokens(q):
    return pl.ds(aligned(q * TOK), TOK)


def kernel(
    x_hbm, g_hbm, u_hbm, c_hbm, other_hbm, out_ref,
    x_v, g_v, u_v, c_v, other_v, gc, cb, cs, xt, xs, ob, acc, gram, pn, fac,
    in_sem, xz_s, xz_r, xa_s, xa_r, yb_s, yb_r, ya_s, ya_r, xb_s, xb_r, ca_s, ca_r, co_s, co_r,
    qa_s, qa_r, rp_s, rp_r, rm_s, rm_r, pn_s, pn_r, fq_s, fq_r, fz_s, fz_r, out_s, out_r, own_s,
):
    dp = lax.axis_index("dp")
    tn = lax.axis_index("tensor")
    z, q = lax.div(dp, Q), lax.rem(dp, Q)
    ylo, core = lax.div(q, 2), lax.rem(q, 2)
    x, yhi = lax.div(tn, 2), lax.rem(tn, 2)
    yy = yhi * 2 + ylo
    xrow = aligned(x * TOK)

    def zq(zd, qd):
        return (zd * Q + qd, tn)

    def x_peer(off):
        return (dp, lax.rem(x + off, XN) * 2 + yhi)

    def y_peer(off):
        to = lax.rem(yy + off, 4)
        return (z * Q + lax.rem(to, 2) * 2 + core, x * 2 + lax.div(to, 2))

    def z_peer(off):
        return zq(lax.rem(z + off, Z), q)

    def q_peer(off):
        return zq(z, lax.rem(q + off, Q))

    def t_peer(off):
        return (dp, lax.rem(tn + off, T))

    core_peer = zq(z, ylo * 2 + 1 - core)

    def remote(src, dst, send, recv, device):
        return pltpu.make_async_remote_copy(
            src_ref=src, dst_ref=dst, send_sem=send, recv_sem=recv,
            device_id=device, device_id_type=MESH,
        )

    loads = [
        pltpu.make_async_copy(src, dst, in_sem.at[i])
        for i, (src, dst) in enumerate(
            ((x_hbm, x_v), (g_hbm, g_v), (u_hbm, u_v), (c_hbm, c_v), (other_hbm, other_v))
        )
    ]
    for load in loads:
        load.start()

    barrier = pltpu.get_barrier_semaphore()

    def greet(device):
        pl.semaphore_signal(barrier, inc=1, device_id=device, device_id_type=MESH)

    for off in range(1, Q):
        greet(q_peer(off))
    for off in range(1, Z):
        greet(z_peer(off))
    for off in range(1, T):
        greet(t_peer(off))
    greet((z * Q + (1 - ylo) * 2 + core, x * 2 + 1 - yhi))

    def quad(j, off):
        to = lax.rem(q + off, Q)
        return remote(
            gc.at[:, pl.ds(aligned(to * PART + j * W), W)], cb.at[j, z, q],
            qa_s.at[j, off], qa_r.at[j, off], q_peer(off),
        )

    def cotangents(j):
        for part in range(Q):
            at = pl.ds(aligned(part * PART + j * W), W)
            gate = g_v[:, at].astype(f32)
            upper = u_v[:, at].astype(f32)
            cotan = c_v[:, at].astype(f32)
            sig = jax.nn.sigmoid(gate)
            slope = sig * (1.0 + gate * (1.0 - sig))
            gc[:, at] = (cotan * upper * slope).astype(bf16)

    def spread(j):
        for off in range(1, Q):
            quad(j, off).start()
        cb[j, z, q] = gc[:, pl.ds(aligned(q * PART + j * W), W)]

    def hop_plus(h, j):
        src = lax.rem(z + Z - (h - 1), Z)
        block = cb.at[j, src] if h < 4 else cb.at[j, src, pl.ds(0, 2)]
        return remote(block, block, rp_s.at[h - 1, j], rp_r.at[h - 1, j], z_peer(1))

    def hop_minus(h, j):
        src = lax.rem(z + (h - 1), Z)
        block = cb.at[j, src] if h < 4 else cb.at[j, src, pl.ds(2, 2)]
        return remote(block, block, rm_s.at[h - 1, j], rm_r.at[h - 1, j], z_peer(Z - 1))

    def first_hop(j):
        for off in range(1, Q):
            quad(j, off).wait_recv()
        hop_plus(1, j).start()
        hop_minus(1, j).start()

    def next_hop(h, j):
        hop_plus(h - 1, j).wait_recv()
        hop_plus(h, j).start()
        hop_minus(h - 1, j).wait_recv()
        hop_minus(h, j).start()

    def turn(zd, _):
        at = aligned(zd * ROWS + yhi * (ROWS // 2) + x * TOK)
        xs[zd] = x_v[:, pl.ds(at, TOK)].T
        return 0

    mine = xt.at[z, yhi, pl.ds(xrow, TOK), tokens(q)]

    def x_z(off):
        return remote(xs.at[lax.rem(z + off, Z)], mine, xz_s.at[off], xz_r.at[off], z_peer(off))

    loads[0].wait()
    lax.fori_loop(0, Z, turn, 0)
    mine[...] = xs[z]
    pl.semaphore_wait(barrier, (Q - 1) + (Z - 1) + (T - 1) + 1)
    for off in (4, 3, 5, 2, 6, 1, 7):
        x_z(off).start()
    for load in loads[1:4]:
        load.wait()
    cotangents(0)
    spread(0)
    cotangents(1)
    spread(1)
    first_hop(0)

    def produce(j, _):
        cotangents(j)
        spread(j)
        first_hop(j - 1)
        return 0

    lax.fori_loop(2, J, produce, 0)
    first_hop(J - 1)

    def x_a(off):
        part = xt.at[A, yhi, pl.ds(xrow, TOK), tokens(q)]
        return remote(part, part, xa_s.at[off], xa_r.at[off], x_peer(off))

    def y_b(off):
        part = xt.at[B, yhi, pl.ds(xrow, TOK), tokens(q)]
        return remote(part, part, yb_s.at[off], yb_r.at[off], y_peer(off))

    def y_a(off):
        part = xt.at[A, yhi, :, tokens(q)]
        return remote(part, part, ya_s.at[off], ya_r.at[off], y_peer(off))

    def x_b(off, lo):
        part = xt.at[B, :, pl.ds(xrow, TOK), tokens(lo * 2 + core)]
        return remote(part, part, xb_s.at[lo, off], xb_r.at[lo, off], x_peer(off))

    def y_far(way):
        src = lax.rem(yy + 4 - way, 4)
        hi, lo = lax.div(src, 2), lax.rem(src, 2)
        at = pl.ds(0 if way == 1 else 2, 2)
        part = xt.at[at, hi, :, tokens(lo * 2 + core)]
        return remote(part, part, ya_s.at[way - 1], ya_r.at[way - 1], y_peer(way))

    def x_far(way, lo):
        row = aligned(lax.rem(x + XN - way, XN) * TOK)
        at = pl.ds(4 if way == 1 else 6, 2)
        part = xt.at[at, :, pl.ds(row, TOK), tokens(lo * 2 + core)]
        return remote(part, part, xb_s.at[lo, way - 1], xb_r.at[lo, way - 1], x_peer(way))

    def swap_a(off):
        src = lax.rem(yy + off, 4)
        hi, lo = lax.div(src, 2), lax.rem(src, 2)
        part = xt.at[A, hi, :, tokens(lo * 2 + core)]
        return remote(part, part, ca_s.at[off], ca_r.at[off], core_peer)

    def swap_b(off, lo):
        row = aligned(lax.rem(x + off, XN) * TOK)
        part = xt.at[B, :, pl.ds(row, TOK), tokens(lo * 2 + core)]
        return remote(part, part, co_s.at[lo, off], co_r.at[lo, off], core_peer)

    for off in range(1, Z):
        x_z(off).wait_recv()
    for off in range(1, XN):
        x_a(off).start()
        y_b(off).start()

    cross = (((1,), (1,)), ((), ()))
    gram[...] = jnp.zeros_like(gram)
    loads[4].wait()

    def gram_x(k, _):
        part = x_v[:, pl.ds(aligned(k * 1024), 1024)]
        gram[0] += lax.dot_general(part, part, cross, preferred_element_type=f32)
        return 0

    lax.fori_loop(0, D // 1024, gram_x, 0)

    def gram_cot(k, _):
        at = pl.ds(aligned(k * 512), 512)
        gate = g_v[:, at].astype(f32)
        upper = (c_v[:, at].astype(f32) * (gate * jax.nn.sigmoid(gate))).astype(bf16)
        gate = gc[:, at]
        gram[1] += lax.dot_general(
            gate, gate, cross, preferred_element_type=f32
        ) + lax.dot_general(upper, upper, cross, preferred_element_type=f32)
        return 0

    lax.fori_loop(0, COLS // 512, gram_cot, 0)

    for e in range(TOK // SEQ):
        at = slice(e * SEQ, (e + 1) * SEQ)
        ghost = jnp.sum(gram[0, at, at] * gram[1, at, at], axis=1, keepdims=True)
        ghost = jnp.sum(ghost, axis=0, keepdims=True)
        rest = jnp.sum(other_v[e : e + 1, :], axis=1, keepdims=True)
        pn[0, e : e + 1, :] = jnp.broadcast_to(ghost + rest, (1, 128))
    pn[0, 2:8, :] = jnp.zeros((6, 128), f32)

    def norms(off):
        return remote(pn.at[0], pn.at[off], pn_s.at[off], pn_r.at[off], t_peer(off))

    for off in range(1, T):
        norms(off).start()

    def factor_q(off):
        return remote(fac.at[z, q], fac.at[z, q], fq_s.at[off], fq_r.at[off], q_peer(off))

    def factor_z(off):
        return remote(fac.at[z], fac.at[z], fz_s.at[off], fz_r.at[off], z_peer(off))

    def second_hop(j, _):
        next_hop(2, j)
        return 0

    for off in range(1, XN):
        y_b(off).wait_recv()
    for off in (1, 3):
        for lo in range(2):
            x_b(off, lo).start()
    lax.fori_loop(0, 1, second_hop, 0)

    for off in range(1, T):
        norms(off).wait_recv()
    total = jnp.zeros((8, 128), f32)
    for t in range(T):
        total = total + pn[lax.rem(tn + T - t, T)]
    fac[z, q] = clip_bound / jnp.maximum(jnp.sqrt(total), clip_bound)
    for off in range(1, Q):
        factor_q(off).start()

    for off in range(1, XN):
        x_a(off).wait_recv()
    for off in (1, 3):
        y_a(off).start()
    swap_a(0).start()
    for lo in range(2):
        swap_b(0, lo).start()
    lax.fori_loop(1, 4, second_hop, 0)

    for off in range(1, Q):
        factor_q(off).wait_recv()
    for off in range(1, Z):
        factor_z(off).start()

    lax.fori_loop(4, J, second_hop, 0)

    for off in (1, 3):
        y_a(off).wait_recv()
        y_far(off).start()
        for lo in range(2):
            x_b(off, lo).wait_recv()
            x_far(off, lo).start()
        swap_a(4 - off).start()
        for lo in range(2):
            swap_b(4 - off, lo).start()

    for off in range(1, Z):
        factor_z(off).wait_recv()

    def scale(j, src):
        at = pl.ds(aligned(j * W), W)
        for part in range(Q):
            for e in range(TOK // SEQ):
                block = cb[j, src, part, e * SEQ : (e + 1) * SEQ, :].astype(f32)
                block = block * fac[src, part, e : e + 1, :]
                cs[src, pl.ds(part * TOK + e * SEQ, SEQ), at] = block.astype(bf16)

    def scale_near(j, _):
        for off in (0, 1, Z - 1):
            scale(j, lax.rem(z + off, Z))
        return 0

    lax.fori_loop(0, J, scale_near, 0)

    def third_hop(j):
        next_hop(3, j)
        for off in (2, Z - 2):
            scale(j, lax.rem(z + off, Z))

    def third_hops(j, _):
        third_hop(j)
        return 0

    lax.fori_loop(0, AHEAD, third_hops, 0)

    for way in (1, 3):
        y_far(way).wait_recv()
        for lo in range(2):
            x_far(way, lo).wait_recv()
    swap_a(2).start()
    for lo in range(2):
        swap_b(2, lo).start()

    def place(j, part):
        return out_ref.at[:, pl.ds(aligned(part * PART + j * W), W)]

    def give(j, off):
        to = lax.rem(q + off, Q)
        return remote(
            ob.at[j, to], place(j, q), out_s.at[j, off], out_r.at[j, off], q_peer(off)
        )

    def keep(j):
        return pltpu.make_async_copy(ob.at[j, q], place(j, q), own_s.at[j])

    def product(half, j, offs):
        at = pl.ds(aligned(j * W), W)
        grad = acc[half, :, at]
        for off in offs:
            src = lax.rem(z + off, Z)
            grad += jnp.dot(xt[src, half], cs[src, :, at], preferred_element_type=f32)
        return grad

    def multiply_near(half, _):
        grad = jnp.dot(xt[z, half], cs[z], preferred_element_type=f32)
        for off in (1, Z - 1):
            src = lax.rem(z + off, Z)
            grad += jnp.dot(xt[src, half], cs[src], preferred_element_type=f32)
        acc[half] = grad
        return 0

    def multiply_early(j):
        for half in range(2):
            acc[half, :, pl.ds(aligned(j * W), W)] = product(half, j, (2, Z - 2, 3, Z - 3))

    def multiply_late(j):
        hop_plus(4, j).wait_recv()
        hop_minus(4, j).wait_recv()
        scale(j, lax.rem(z + 4, Z))
        for half in range(2):
            grad = product(half, j, (4,)).astype(bf16)
            ob[j, 2 * half] = grad[:OWN]
            ob[j, 2 * half + 1] = grad[OWN:]
        for off in range(1, Q):
            give(j, off).start()
        keep(j).start()

    for off in range(Q):
        swap_a(off).wait_recv()
        for lo in range(2):
            swap_b(off, lo).wait_recv()
    lax.fori_loop(0, 2, multiply_near, 0)

    def last_hops(i, _):
        @pl.when((i + LAG >= AHEAD) & (i + LAG < J))
        def _():
            third_hop(i + LAG)

        @pl.when(i < J)
        def _():
            next_hop(4, i)
            for off in (3, Z - 3):
                scale(i, lax.rem(z + off, Z))

        @pl.when(i > 0)
        def _():
            multiply_late(i - 1)

        @pl.when(i < J)
        def _():
            multiply_early(i)

        return 0

    lax.fori_loop(0, J + 1, last_hops, 0)

    for off in range(1, Z):
        x_z(off).wait_send()
        factor_z(off).wait_send()
    for off in range(1, T):
        norms(off).wait_send()
    for off in range(1, Q):
        x_a(off).wait_send()
        y_b(off).wait_send()
        factor_q(off).wait_send()
    for off in (1, 3):
        y_a(off).wait_send()
        y_far(off).wait_send()
        for lo in range(2):
            x_b(off, lo).wait_send()
            x_far(off, lo).wait_send()
    for off in range(Q):
        swap_a(off).wait_send()
        for lo in range(2):
            swap_b(off, lo).wait_send()

    def finish(j, _):
        for off in range(1, Q):
            quad(j, off).wait_send()
        for h in range(1, 5):
            hop_plus(h, j).wait_send()
            hop_minus(h, j).wait_send()
        for off in range(1, Q):
            give(j, off).wait_send()
            give(j, off).wait_recv()
        keep(j).wait()
        return 0

    lax.fori_loop(0, J, finish, 0)


def shards(layer_input, gate_pre, up_pre, hidden_cot, other_norms, noise_gate):
    dma = pltpu.SemaphoreType.DMA
    anywhere = pl.BlockSpec(memory_space=pl.ANY)
    grad = pl.pallas_call(
        kernel,
        out_shape=jax.ShapeDtypeStruct((OWN, COLS), bf16),
        in_specs=[anywhere] * 5,
        out_specs=anywhere,
        scratch_shapes=[
            pltpu.VMEM((TOK, D), bf16),
            pltpu.VMEM((TOK, COLS), bf16),
            pltpu.VMEM((TOK, COLS), bf16),
            pltpu.VMEM((TOK, COLS), bf16),
            pltpu.VMEM((2, 16), f32),
            pltpu.VMEM((TOK, COLS), bf16),
            pltpu.VMEM((J, Z, Q, TOK, W), bf16),
            pltpu.VMEM((Z, Q * TOK, PART), bf16),
            pltpu.VMEM((Z, 2, ROWS // 2, Q * TOK), bf16),
            pltpu.VMEM((Z, TOK, TOK), bf16),
            pltpu.VMEM((J, Q, OWN, W), bf16),
            pltpu.VMEM((2, ROWS // 2, PART), f32),
            pltpu.VMEM((2, TOK, TOK), f32),
            pltpu.VMEM((T, 8, 128), f32),
            pltpu.VMEM((Z, Q, 8, 128), f32),
            dma((5,)),
            dma((Z,)), dma((Z,)),
            dma((4,)), dma((4,)), dma((4,)), dma((4,)), dma((4,)), dma((4,)),
            dma((2, 4)), dma((2, 4)), dma((4,)), dma((4,)), dma((2, 4)), dma((2, 4)),
            dma((J, Q)), dma((J, Q)),
            dma((4, J)), dma((4, J)), dma((4, J)), dma((4, J)),
            dma((T,)), dma((T,)), dma((Q,)), dma((Q,)), dma((Z,)), dma((Z,)),
            dma((J, Q)), dma((J, Q)), dma((J,)),
        ],
        compiler_params=pltpu.CompilerParams(
            collective_id=0, has_side_effects=True, vmem_limit_bytes=40 * 1024 * 1024
        ),
        cost_estimate=pl.CostEstimate(
            flops=2 * 4096 * 256 * 3584, bytes_accessed=8 * 1024 * 1024, transcendentals=128 * 3584
        ),
        name="clipped_gradient",
    )(*(pltpu.with_memory_space_constraint(a, pltpu.HBM) for a in (layer_input, gate_pre, up_pre, hidden_cot, other_norms)))
    return grad.astype(f32) + noise_gate.astype(f32)


def solution(mesh):
    placed = (
        P("dp", None),
        P("dp", "tensor"),
        P("dp", "tensor"),
        P("dp", "tensor"),
        P("dp", "tensor"),
        P("dp", "tensor"),
    )
    return jax.shard_map(
        shards, mesh=mesh, in_specs=placed, out_specs=P("dp", "tensor"), check_vma=False
    )
```

time: 114 us -> 103 us (0.904)
  Pallas kernels: 110 us -> 101 us
  other arithmetic: 3.86 us -> 2.36 us
    pallas_call x1, Pallas kernels: 110 us -> 101 us  [shards(): pl.pallas_call(kernel, out_shape=jax.ShapeDtypeStruct((OWN, COLS), bf16),...]
    add x1, other arithmetic: 3.86 us -> 2.36 us  [shards(): return grad.astype(f32) + noise_gate.astype(f32)]
where the time goes in v2:
time: 103 us
  Pallas kernels  101 us (98%)
  other arithmetic  2.36 us (2%)
    pallas_call x1, Pallas kernels, shards(): pl.pallas_call(kernel, out_shape=jax.ShapeDtypeStruct((OWN, COLS), bf16),...  101 us
    add x1, other arithmetic, shards(): return grad.astype(f32) + noise_gate.astype(f32)  2.36 us

profile of v2, /device:TPU:1, one launch (start us, length us, event | category | flops | bytes accessed | tf_op | source)
XLA Modules:
  0.0 103.1 jit_solution(12441415308986639965)
XLA Ops:
  0.0 0.0 copy-start
  0.0 100.7 %clipped_gradient.1 = bf16[256,3584]{1,0:T(8,128)(2,1)S(1)} custom-call(bf16[128,8192]{1,0:T(8,128)(2,1)} %x_hbm.1, bf16[128,3584]{1,0:T(8,128)(2,1)} %g_hbm.1, bf16[128,3584]{1,0:T(8,128)(2,1)} %u_hbm.1, bf16[128,3584]{1,0:T(8,128)(2,1)} %c_hbm.1, f32[2,16]{1,0:T(2,128)} %other_hbm.1), custom_call_target="tpu_custom_call" | custom-call | flops 7516192768 | bytes 8388608 | tf_op jit(solution)/shard_map/clipped_gradient/pallas_call | solution.py:466
  100.7 0.0 copy-done
  100.7 2.4 %convert_add_fusion = f32[256,3584]{1,0:T(8,128)} fusion(bf16[256,3584]{1,0:T(8,128)(2,1)S(1)} %copy-done, bf16[256,3584]{1,0:T(8,128)(2,1)S(1)} %clipped_gradient.1), kind=kLoop, calls=%fused_computation | loop fusion | flops 2752512 | bytes 7340032 | tf_op jit(solution)/shard_map/add | solution.py:504
Async XLA Ops:
  0.0 100.7 %copy-start = (bf16[256,3584]{1,0:T(8,128)(2,1)S(1)}, bf16[256,3584]{1,0:T(8,128)(2,1)}, u32[]{:S(2)}) copy-start(bf16[256,3584]{1,0:T(8,128)(2,1)} %param.11) | copy-start | bytes 5505028

commit v3 on v2

--- a/solution.py
+++ b/solution.py
@@ -25,8 +25,7 @@
 ROWS = 1024
 OWN = ROWS // Q
 A, B = pl.ds(0, Z // 2), pl.ds(Z // 2, Z // 2)
-LAG = 2
-AHEAD = 3
+AHEAD = 2
 MESH = pl.DeviceIdType.MESH
 f32 = jnp.float32
 bf16 = jnp.bfloat16
@@ -42,8 +41,8 @@
 
 def kernel(
     x_hbm, g_hbm, u_hbm, c_hbm, other_hbm, out_ref,
-    x_v, g_v, u_v, c_v, other_v, gc, cb, cs, xt, xs, ob, acc, gram, pn, fac,
-    in_sem, xz_s, xz_r, xa_s, xa_r, yb_s, yb_r, ya_s, ya_r, xb_s, xb_r, ca_s, ca_r, co_s, co_r,
+    x_v, g_v, u_v, c_v, other_v, gc, cb, cs, xt, xc, xs, ob, acc, gram, pn, fac,
+    in_sem, slice_sem, xz_s, xz_r, xa_s, xa_r, yb_s, yb_r, ya_s, ya_r, xb_s, xb_r, ca_s, ca_r, co_s, co_r,
     qa_s, qa_r, rp_s, rp_r, rm_s, rm_r, pn_s, pn_r, fq_s, fq_r, fz_s, fz_r, out_s, out_r, own_s,
 ):
     dp = lax.axis_index("dp")
@@ -84,9 +83,16 @@
     loads = [
         pltpu.make_async_copy(src, dst, in_sem.at[i])
         for i, (src, dst) in enumerate(
-            ((x_hbm, x_v), (g_hbm, g_v), (u_hbm, u_v), (c_hbm, c_v), (other_hbm, other_v))
+            ((g_hbm, g_v), (u_hbm, u_v), (c_hbm, c_v), (x_hbm, x_v), (other_hbm, other_v))
         )
     ]
+
+    def slice_of(zd):
+        at = pl.ds(aligned(zd * ROWS + yhi * (ROWS // 2) + x * TOK), TOK)
+        return pltpu.make_async_copy(x_hbm.at[:, at], xc.at[zd], slice_sem.at[zd])
+
+    for zd in range(Z):
+        slice_of(zd).start()
     for load in loads:
         load.start()
 
@@ -126,13 +132,17 @@
         cb[j, z, q] = gc[:, pl.ds(aligned(q * PART + j * W), W)]
 
     def hop_plus(h, j):
-        src = lax.rem(z + Z - (h - 1), Z)
-        block = cb.at[j, src] if h < 4 else cb.at[j, src, pl.ds(0, 2)]
+        src = lax.rem(z + Z - {1: 0, 2: 1, 3: 2, 4: 3, 5: 2}[h], Z)
+        block = cb.at[j, src]
+        if h > 2:
+            block = cb.at[j, src, pl.ds(2 if h == 5 else 0, 2)]
         return remote(block, block, rp_s.at[h - 1, j], rp_r.at[h - 1, j], z_peer(1))
 
     def hop_minus(h, j):
-        src = lax.rem(z + (h - 1), Z)
-        block = cb.at[j, src] if h < 4 else cb.at[j, src, pl.ds(2, 2)]
+        src = lax.rem(z + {1: 0, 2: 1, 3: 2, 4: 3, 5: 2}[h], Z)
+        block = cb.at[j, src]
+        if h > 2:
+            block = cb.at[j, src, pl.ds(0 if h == 5 else 2, 2)]
         return remote(block, block, rm_s.at[h - 1, j], rm_r.at[h - 1, j], z_peer(Z - 1))
 
     def first_hop(j):
@@ -148,8 +158,7 @@
         hop_minus(h, j).start()
 
     def turn(zd, _):
-        at = aligned(zd * ROWS + yhi * (ROWS // 2) + x * TOK)
-        xs[zd] = x_v[:, pl.ds(at, TOK)].T
+        xs[zd] = xc[zd].T
         return 0
 
     mine = xt.at[z, yhi, pl.ds(xrow, TOK), tokens(q)]
@@ -157,13 +166,14 @@
     def x_z(off):
         return remote(xs.at[lax.rem(z + off, Z)], mine, xz_s.at[off], xz_r.at[off], z_peer(off))
 
-    loads[0].wait()
+    for zd in range(Z):
+        slice_of(zd).wait()
     lax.fori_loop(0, Z, turn, 0)
     mine[...] = xs[z]
     pl.semaphore_wait(barrier, (Q - 1) + (Z - 1) + (T - 1) + 1)
     for off in (4, 3, 5, 2, 6, 1, 7):
         x_z(off).start()
-    for load in loads[1:4]:
+    for load in loads[:3]:
         load.wait()
     cotangents(0)
     spread(0)
@@ -228,6 +238,7 @@
 
     cross = (((1,), (1,)), ((), ()))
     gram[...] = jnp.zeros_like(gram)
+    loads[3].wait()
     loads[4].wait()
 
     def gram_x(k, _):
@@ -335,6 +346,11 @@
 
     def third_hop(j):
         next_hop(3, j)
+        rest_of_third(j)
+
+    def rest_of_third(j):
+        hop_plus(5, j).start()
+        hop_minus(5, j).start()
         for off in (2, Z - 2):
             scale(j, lax.rem(z + off, Z))
 
@@ -403,27 +419,35 @@
     lax.fori_loop(0, 2, multiply_near, 0)
 
     def last_hops(i, _):
-        @pl.when((i + LAG >= AHEAD) & (i + LAG < J))
+        more = (i >= AHEAD) & (i < J)
+
+        @pl.when(more)
         def _():
-            third_hop(i + LAG)
-
-        @pl.when(i < J)
+            next_hop(3, i)
+
+        @pl.when(i <= J)
         def _():
-            next_hop(4, i)
+            next_hop(4, i - 1)
+
+        @pl.when(more)
+        def _():
+            rest_of_third(i)
+
+        @pl.when(i > 1)
+        def _():
+            multiply_late(i - 2)
+
+        @pl.when(i <= J)
+        def _():
+            hop_plus(5, i - 1).wait_recv()
+            hop_minus(5, i - 1).wait_recv()
             for off in (3, Z - 3):
-                scale(i, lax.rem(z + off, Z))
-
-        @pl.when(i > 0)
-        def _():
-            multiply_late(i - 1)
-
-        @pl.when(i < J)
-        def _():
-            multiply_early(i)
-
-        return 0
-
-    lax.fori_loop(0, J + 1, last_hops, 0)
+                scale(i - 1, lax.rem(z + off, Z))
+            multiply_early(i - 1)
+
+        return 0
+
+    lax.fori_loop(1, J + 2, last_hops, 0)
 
     for off in range(1, Z):
         x_z(off).wait_send()
@@ -448,7 +472,7 @@
     def finish(j, _):
         for off in range(1, Q):
             quad(j, off).wait_send()
-        for h in range(1, 5):
+        for h in range(1, 6):
             hop_plus(h, j).wait_send()
             hop_minus(h, j).wait_send()
         for off in range(1, Q):
@@ -479,17 +503,18 @@
             pltpu.VMEM((Z, Q * TOK, PART), bf16),
             pltpu.VMEM((Z, 2, ROWS // 2, Q * TOK), bf16),
             pltpu.VMEM((Z, TOK, TOK), bf16),
+            pltpu.VMEM((Z, TOK, TOK), bf16),
             pltpu.VMEM((J, Q, OWN, W), bf16),
             pltpu.VMEM((2, ROWS // 2, PART), f32),
             pltpu.VMEM((2, TOK, TOK), f32),
             pltpu.VMEM((T, 8, 128), f32),
             pltpu.VMEM((Z, Q, 8, 128), f32),
-            dma((5,)),
+            dma((5,)), dma((Z,)),
             dma((Z,)), dma((Z,)),
             dma((4,)), dma((4,)), dma((4,)), dma((4,)), dma((4,)), dma((4,)),
             dma((2, 4)), dma((2, 4)), dma((4,)), dma((4,)), dma((2, 4)), dma((2, 4)),
             dma((J, Q)), dma((J, Q)),
-            dma((4, J)), dma((4, J)), dma((4, J)), dma((4, J)),
+            dma((5, J)), dma((5, J)), dma((5, J)), dma((5, J)),
             dma((T,)), dma((T,)), dma((Q,)), dma((Q,)), dma((Z,)), dma((Z,)),
             dma((J, Q)), dma((J, Q)), dma((J,)),
         ],

time: 103 us -> 101 us (0.981)
  Pallas kernels: 101 us -> 98.6 us
    pallas_call x1, Pallas kernels: 101 us -> 98.6 us  [shards(): pl.pallas_call(kernel, out_shape=jax.ShapeDtypeStruct((OWN, COLS), bf16),...]
where the time goes in v3:
time: 101 us
  Pallas kernels  98.6 us (98%)
  other arithmetic  2.36 us (2%)
    pallas_call x1, Pallas kernels, shards(): pl.pallas_call(kernel, out_shape=jax.ShapeDtypeStruct((OWN, COLS), bf16),...  98.6 us
    add x1, other arithmetic, shards(): return grad.astype(f32) + noise_gate.astype(f32)  2.36 us

profile of v3, /device:TPU:1, one launch (start us, length us, event | category | flops | bytes accessed | tf_op | source)
XLA Modules:
  0.0 100.9 jit_solution(7369731503557287086)
XLA Ops:
  0.0 0.0 copy-start
  0.0 98.6 %clipped_gradient.1 = bf16[256,3584]{1,0:T(8,128)(2,1)S(1)} custom-call(bf16[128,8192]{1,0:T(8,128)(2,1)} %x_hbm.1, bf16[128,3584]{1,0:T(8,128)(2,1)} %g_hbm.1, bf16[128,3584]{1,0:T(8,128)(2,1)} %u_hbm.1, bf16[128,3584]{1,0:T(8,128)(2,1)} %c_hbm.1, f32[2,16]{1,0:T(2,128)} %other_hbm.1), custom_call_target="tpu_custom_call" | custom-call | flops 7516192768 | bytes 8388608 | tf_op jit(solution)/shard_map/clipped_gradient/pallas_call | solution.py:490
  98.6 0.0 copy-done
  98.6 2.4 %convert_add_fusion = f32[256,3584]{1,0:T(8,128)} fusion(bf16[256,3584]{1,0:T(8,128)(2,1)S(1)} %copy-done, bf16[256,3584]{1,0:T(8,128)(2,1)S(1)} %clipped_gradient.1), kind=kLoop, calls=%fused_computation | loop fusion | flops 2752512 | bytes 7340032 | tf_op jit(solution)/shard_map/add | solution.py:529
Async XLA Ops:
  0.0 98.6 %copy-start = (bf16[256,3584]{1,0:T(8,128)(2,1)S(1)}, bf16[256,3584]{1,0:T(8,128)(2,1)}, u32[]{:S(2)}) copy-start(bf16[256,3584]{1,0:T(8,128)(2,1)} %param.11) | copy-start | bytes 5505028

commit v4 on v3

--- a/solution.py
+++ b/solution.py
@@ -41,7 +41,7 @@
 
 def kernel(
     x_hbm, g_hbm, u_hbm, c_hbm, other_hbm, out_ref,
-    x_v, g_v, u_v, c_v, other_v, gc, cb, cs, xt, xc, xs, ob, acc, gram, pn, fac,
+    x_v, g_v, u_v, c_v, other_v, gc, cb, cs, xt, xc, xs, ob, acc, gram, pn, fq, fac,
     in_sem, slice_sem, xz_s, xz_r, xa_s, xa_r, yb_s, yb_r, ya_s, ya_r, xb_s, xb_r, ca_s, ca_r, co_s, co_r,
     qa_s, qa_r, rp_s, rp_r, rm_s, rm_r, pn_s, pn_r, fq_s, fq_r, fz_s, fz_r, out_s, out_r, own_s,
 ):
@@ -275,7 +275,7 @@
         norms(off).start()
 
     def factor_q(off):
-        return remote(fac.at[z, q], fac.at[z, q], fq_s.at[off], fq_r.at[off], q_peer(off))
+        return remote(fq.at[q], fq.at[q], fq_s.at[off], fq_r.at[off], q_peer(off))
 
     def factor_z(off):
         return remote(fac.at[z], fac.at[z], fz_s.at[off], fz_r.at[off], z_peer(off))
@@ -296,7 +296,7 @@
     total = jnp.zeros((8, 128), f32)
     for t in range(T):
         total = total + pn[lax.rem(tn + T - t, T)]
-    fac[z, q] = clip_bound / jnp.maximum(jnp.sqrt(total), clip_bound)
+    fq[q] = clip_bound / jnp.maximum(jnp.sqrt(total), clip_bound)
     for off in range(1, Q):
         factor_q(off).start()
 
@@ -311,6 +311,8 @@
 
     for off in range(1, Q):
         factor_q(off).wait_recv()
+    for part in range(Q):
+        fac[z, 2 * part : 2 * part + 2, :] = fq[part, 0:2, :]
     for off in range(1, Z):
         factor_z(off).start()
 
@@ -334,7 +336,7 @@
         for part in range(Q):
             for e in range(TOK // SEQ):
                 block = cb[j, src, part, e * SEQ : (e + 1) * SEQ, :].astype(f32)
-                block = block * fac[src, part, e : e + 1, :]
+                block = block * fac[src, 2 * part + e : 2 * part + e + 1, :]
                 cs[src, pl.ds(part * TOK + e * SEQ, SEQ), at] = block.astype(bf16)
 
     def scale_near(j, _):
@@ -508,7 +510,8 @@
             pltpu.VMEM((2, ROWS // 2, PART), f32),
             pltpu.VMEM((2, TOK, TOK), f32),
             pltpu.VMEM((T, 8, 128), f32),
-            pltpu.VMEM((Z, Q, 8, 128), f32),
+            pltpu.VMEM((Q, 8, 128), f32),
+            pltpu.VMEM((Z, 8, 128), f32),
             dma((5,)), dma((Z,)),
             dma((Z,)), dma((Z,)),
             dma((4,)), dma((4,)), dma((4,)), dma((4,)), dma((4,)), dma((4,)),

time: 101 us -> 98.9 us (0.979)
  Pallas kernels: 98.6 us -> 96.4 us
    pallas_call x1, Pallas kernels: 98.6 us -> 96.4 us  [shards(): pl.pallas_call(kernel, out_shape=jax.ShapeDtypeStruct((OWN, COLS), bf16),...]
where the time goes in v4:
time: 98.9 us; the launch traced here: 98.8 us
  Pallas kernels  96.4 us (97%)
  other arithmetic  2.36 us (2%)
    pallas_call x1, Pallas kernels, shards(): pl.pallas_call(kernel, out_shape=jax.ShapeDtypeStruct((OWN, COLS), bf16),...  96.4 us
    add x1, other arithmetic, shards(): return grad.astype(f32) + noise_gate.astype(f32)  2.36 us

profile of v4, /device:TPU:1, one launch (start us, length us, event | category | flops | bytes accessed | tf_op | source)
XLA Modules:
  0.0 98.8 jit_solution(2281972439626025911)
XLA Ops:
  0.0 0.0 copy-start
  0.0 96.4 %clipped_gradient.1 = bf16[256,3584]{1,0:T(8,128)(2,1)S(1)} custom-call(bf16[128,8192]{1,0:T(8,128)(2,1)} %x_hbm.1, bf16[128,3584]{1,0:T(8,128)(2,1)} %g_hbm.1, bf16[128,3584]{1,0:T(8,128)(2,1)} %u_hbm.1, bf16[128,3584]{1,0:T(8,128)(2,1)} %c_hbm.1, f32[2,16]{1,0:T(2,128)} %other_hbm.1), custom_call_target="tpu_custom_call" | custom-call | flops 7516192768 | bytes 8388608 | tf_op jit(solution)/shard_map/clipped_gradient/pallas_call | solution.py:492
  96.4 0.0 copy-done
  96.4 2.4 %convert_add_fusion = f32[256,3584]{1,0:T(8,128)} fusion(bf16[256,3584]{1,0:T(8,128)(2,1)S(1)} %copy-done, bf16[256,3584]{1,0:T(8,128)(2,1)S(1)} %clipped_gradient.1), kind=kLoop, calls=%fused_computation | loop fusion | flops 2752512 | bytes 7340032 | tf_op jit(solution)/shard_map/add | solution.py:532
Async XLA Ops:
  0.0 96.4 %copy-start = (bf16[256,3584]{1,0:T(8,128)(2,1)S(1)}, bf16[256,3584]{1,0:T(8,128)(2,1)}, u32[]{:S(2)}) copy-start(bf16[256,3584]{1,0:T(8,128)(2,1)} %param.11) | copy-start | bytes 5505028

commit v5 on v4

--- a/solution.py
+++ b/solution.py
@@ -178,8 +178,8 @@
     cotangents(0)
     spread(0)
     cotangents(1)
+    first_hop(0)
     spread(1)
-    first_hop(0)
 
     def produce(j, _):
         cotangents(j)
@@ -307,8 +307,6 @@
     swap_a(0).start()
     for lo in range(2):
         swap_b(0, lo).start()
-    lax.fori_loop(1, 4, second_hop, 0)
-
     for off in range(1, Q):
         factor_q(off).wait_recv()
     for part in range(Q):
@@ -316,7 +314,7 @@
     for off in range(1, Z):
         factor_z(off).start()
 
-    lax.fori_loop(4, J, second_hop, 0)
+    lax.fori_loop(1, J, second_hop, 0)
 
     for off in (1, 3):
         y_a(off).wait_recv()
@@ -327,6 +325,17 @@
         swap_a(4 - off).start()
         for lo in range(2):
             swap_b(4 - off, lo).start()
+
+    def rest_of_third(j):
+        hop_plus(5, j).start()
+        hop_minus(5, j).start()
+
+    def third_hops(j, _):
+        next_hop(3, j)
+        rest_of_third(j)
+        return 0
+
+    lax.fori_loop(0, AHEAD, third_hops, 0)
 
     for off in range(1, Z):
         factor_z(off).wait_recv()
@@ -346,21 +355,15 @@
 
     lax.fori_loop(0, J, scale_near, 0)
 
-    def third_hop(j):
-        next_hop(3, j)
-        rest_of_third(j)
-
-    def rest_of_third(j):
-        hop_plus(5, j).start()
-        hop_minus(5, j).start()
+    def scale_second(j):
         for off in (2, Z - 2):
             scale(j, lax.rem(z + off, Z))
 
-    def third_hops(j, _):
-        third_hop(j)
-        return 0
-
-    lax.fori_loop(0, AHEAD, third_hops, 0)
+    def scale_seconds(j, _):
+        scale_second(j)
+        return 0
+
+    lax.fori_loop(0, AHEAD, scale_seconds, 0)
 
     for way in (1, 3):
         y_far(way).wait_recv()
@@ -434,6 +437,7 @@
         @pl.when(more)
         def _():
             rest_of_third(i)
+            scale_second(i)
 
         @pl.when(i > 1)
         def _():

time: 98.9 us -> 99.5 us (level)
  no operation moved by 1% of the time
where the time goes in v5:
time: 99.5 us; the launch traced here: 99.4 us
  Pallas kernels  97 us (97%)
  other arithmetic  2.36 us (2%)
    pallas_call x1, Pallas kernels, shards(): pl.pallas_call(kernel, out_shape=jax.ShapeDtypeStruct((OWN, COLS), bf16),...  97 us
    add x1, other arithmetic, shards(): return grad.astype(f32) + noise_gate.astype(f32)  2.36 us

profile of v5, /device:TPU:1, one launch (start us, length us, event | category | flops | bytes accessed | tf_op | source)
XLA Modules:
  0.0 99.4 jit_solution(3095183061128245663)
XLA Ops:
  0.0 0.0 copy-start
  0.0 97.0 %clipped_gradient.1 = bf16[256,3584]{1,0:T(8,128)(2,1)S(1)} custom-call(bf16[128,8192]{1,0:T(8,128)(2,1)} %x_hbm.1, bf16[128,3584]{1,0:T(8,128)(2,1)} %g_hbm.1, bf16[128,3584]{1,0:T(8,128)(2,1)} %u_hbm.1, bf16[128,3584]{1,0:T(8,128)(2,1)} %c_hbm.1, f32[2,16]{1,0:T(2,128)} %other_hbm.1), custom_call_target="tpu_custom_call" | custom-call | flops 7516192768 | bytes 8388608 | tf_op jit(solution)/shard_map/clipped_gradient/pallas_call | solution.py:496
  97.0 0.0 copy-done
  97.0 2.4 %convert_add_fusion = f32[256,3584]{1,0:T(8,128)} fusion(bf16[256,3584]{1,0:T(8,128)(2,1)S(1)} %copy-done, bf16[256,3584]{1,0:T(8,128)(2,1)S(1)} %clipped_gradient.1), kind=kLoop, calls=%fused_computation | loop fusion | flops 2752512 | bytes 7340032 | tf_op jit(solution)/shard_map/add | solution.py:536
Async XLA Ops:
  0.0 97.0 %copy-start = (bf16[256,3584]{1,0:T(8,128)(2,1)S(1)}, bf16[256,3584]{1,0:T(8,128)(2,1)}, u32[]{:S(2)}) copy-start(bf16[256,3584]{1,0:T(8,128)(2,1)} %param.11) | copy-start | bytes 5505028

commit v6 on v4

--- a/solution.py
+++ b/solution.py
@@ -406,12 +406,12 @@
         hop_plus(4, j).wait_recv()
         hop_minus(4, j).wait_recv()
         scale(j, lax.rem(z + 4, Z))
-        for half in range(2):
+        for half, offs in ((1 - ylo, (2, 3 - 2 * core)), (ylo, (1 + 2 * core,))):
             grad = product(half, j, (4,)).astype(bf16)
             ob[j, 2 * half] = grad[:OWN]
             ob[j, 2 * half + 1] = grad[OWN:]
-        for off in range(1, Q):
-            give(j, off).start()
+            for off in offs:
+                give(j, off).start()
         keep(j).start()
 
     for off in range(Q):

time: 98.9 us -> 98.7 us (level)
  no operation moved by 1% of the time
where the time goes in v6:
time: 98.7 us; the launch traced here: 98.6 us
  Pallas kernels  96.3 us (98%)
  other arithmetic  2.36 us (2%)
    pallas_call x1, Pallas kernels, shards(): pl.pallas_call(kernel, out_shape=jax.ShapeDtypeStruct((OWN, COLS), bf16),...  96.3 us
    add x1, other arithmetic, shards(): return grad.astype(f32) + noise_gate.astype(f32)  2.36 us

profile of v6, /device:TPU:1, one launch (start us, length us, event | category | flops | bytes accessed | tf_op | source)
XLA Modules:
  0.0 98.6 jit_solution(3597396737376992252)
XLA Ops:
  0.0 0.0 copy-start
  0.0 96.3 %clipped_gradient.1 = bf16[256,3584]{1,0:T(8,128)(2,1)S(1)} custom-call(bf16[128,8192]{1,0:T(8,128)(2,1)} %x_hbm.1, bf16[128,3584]{1,0:T(8,128)(2,1)} %g_hbm.1, bf16[128,3584]{1,0:T(8,128)(2,1)} %u_hbm.1, bf16[128,3584]{1,0:T(8,128)(2,1)} %c_hbm.1, f32[2,16]{1,0:T(2,128)} %other_hbm.1), custom_call_target="tpu_custom_call" | custom-call | flops 7516192768 | bytes 8388608 | tf_op jit(solution)/shard_map/clipped_gradient/pallas_call | solution.py:492
  96.3 0.0 copy-done
  96.3 2.4 %convert_add_fusion = f32[256,3584]{1,0:T(8,128)} fusion(bf16[256,3584]{1,0:T(8,128)(2,1)S(1)} %copy-done, bf16[256,3584]{1,0:T(8,128)(2,1)S(1)} %clipped_gradient.1), kind=kLoop, calls=%fused_computation | loop fusion | flops 2752512 | bytes 7340032 | tf_op jit(solution)/shard_map/add | solution.py:532
Async XLA Ops:
  0.0 96.3 %copy-start = (bf16[256,3584]{1,0:T(8,128)(2,1)S(1)}, bf16[256,3584]{1,0:T(8,128)(2,1)}, u32[]{:S(2)}) copy-start(bf16[256,3584]{1,0:T(8,128)(2,1)} %param.11) | copy-start | bytes 5505028
